TPU v7x, 512 devices: a whole 4x8x8 slice. The times are simulated.
512 devices in a mesh: loop: 16 (over y, x_hi), dp: 32 (over z, x_lo, core).
Axes of the slice: x: 4 (x_hi: 2, x_lo: 2; x = x_hi * 2 + x_lo), y: 8, z: 8, core: 2. Of those that a mesh axis runs over, the one named last changes fastest.
Arguments:
- images: bfloat16 [32, 32, 16, 16, 768], P('dp', 'loop'), may hold values from -6 to 6
- kernel: float32 [7, 7, 768], replicated, may hold values from -0.875 to 0.875
- ln_gain: float32 [768], replicated, may hold values from 0.5 to 1.5
- w_up: bfloat16 [768, 1536], P('dp'), may hold values from -0.21875 to 0.21875
- b_up: float32 [1536], replicated, may hold values from -3 to 3
- w_down: bfloat16 [1536, 768], P('dp'), may hold values from -0.15625 to 0.15625
- layer_scale: float32 [768], replicated, may hold values from 0.3 to 1
- w_head: bfloat16 [768, 1152], P('dp'), may hold values from -0.21875 to 0.21875
- text_rows: bfloat16 [32, 32, 1152], P('dp', 'loop'), may hold values from -6 to 6
- pair_ids: int32 [32, 32], P('dp', 'loop'), may hold values from 0 to 31, each once within a row
- log_temp: float32 [1], replicated, may hold values from 1.5 to 2.5
- loss_bias: float32 [1], replicated, may hold values from -6 to -2
Outputs:
- kernel_grad: float32 [7, 7, 768], replicated
- up_grad: float32 [768, 1536], P('dp')
- text_grad: float32 [32, 32, 1152], P('dp', 'loop')
Inputs may be any that keep to these rules, and one draw needn't show every extreme that they name: Each row of pair_ids holds every index of its group once.
All inputs are finite; a program needn't handle non-finite values.
Results may differ from a plain program's by a relative error of at most 0.04.
Values may be sent and summed in bfloat16 or wider, within the bound.
A program may use at most 64 MiB of HBM per device.

v0:
```python
import jax
import jax.numpy as jnp
from jax import lax
from jax.sharding import PartitionSpec as P

epsilon = 1e-06


def passed_along(value, axis, steps):
    count = lax.axis_size(axis)
    pairs = [(source, (source + steps) % count) for source in range(count)]
    return lax.ppermute(value, axis, pairs)


def image_tower(kernel, w_up, images, ln_gain, b_up, w_down, layer_scale, w_head):
    image_count = images.shape[0]
    grid_side = images.shape[1]
    channels = images.shape[3]
    padded = jnp.pad(images, ((0, 0), (3, 3), (3, 3), (0, 0)))
    conv_out = jnp.zeros(images.shape, jnp.float32)
    for row_off in range(7):
        for col_off in range(7):
            window = padded[:, row_off : row_off + grid_side, col_off : col_off + grid_side, :]
            conv_out = conv_out + window.astype(jnp.float32) * kernel[row_off, col_off]
    chan_mean = jnp.mean(conv_out, axis=-1, keepdims=True)
    centered = conv_out - chan_mean
    chan_var = jnp.mean(centered * centered, axis=-1, keepdims=True)
    normed = (centered * lax.rsqrt(chan_var + epsilon) * ln_gain).astype(jnp.bfloat16)
    flat_rows = normed.reshape(-1, channels)
    hidden = jnp.dot(flat_rows, w_up, preferred_element_type=jnp.float32) + b_up
    active = jax.nn.gelu(hidden, approximate=True).astype(jnp.bfloat16)
    mlp_out = jnp.dot(active, w_down, preferred_element_type=jnp.float32)
    block_out = images.reshape(-1, channels).astype(jnp.float32) + layer_scale * mlp_out
    pooled = jnp.mean(
        block_out.reshape(image_count, grid_side * grid_side, channels), axis=1
    ).astype(jnp.bfloat16)
    embedding = jnp.dot(pooled, w_head, preferred_element_type=jnp.float32)
    return embedding * lax.rsqrt(jnp.sum(embedding * embedding, axis=-1, keepdims=True) + epsilon)


def pair_grad(image_emb, text_emb, pair_row, text_index, logit_scale, logit_bias, group_size):
    logits = (
        logit_scale * jnp.dot(image_emb, text_emb.T, precision=lax.Precision.HIGHEST) + logit_bias
    )
    sign_of = jnp.where(pair_row[:, None] == text_index[None, :], 1.0, -1.0)
    return -sign_of * jax.nn.sigmoid(-sign_of * logits) / group_size


def body(
    images,
    kernel,
    ln_gain,
    w_up,
    b_up,
    w_down,
    layer_scale,
    w_head,
    text_rows,
    pair_ids,
    log_temp,
    loss_bias,
):
    loop_size = lax.axis_size("loop")
    loop_index = lax.axis_index("loop")
    up_full, down_full, head_full = (
        lax.all_gather(w_up, "dp", axis=0, tiled=True),
        lax.all_gather(w_down, "dp", axis=0, tiled=True),
        lax.all_gather(w_head, "dp", axis=0, tiled=True),
    )
    pictures = images[0]
    pair_row = pair_ids[0]
    img_dev = pictures.shape[0]
    group_size = img_dev * loop_size
    logit_scale = jnp.exp(log_temp[0])
    logit_bias = loss_bias[0]

    def run_tower(kernel_arg, up_arg):
        return image_tower(
            kernel_arg, up_arg, pictures, ln_gain, b_up, down_full, layer_scale, head_full
        )

    image_emb, pullback = jax.vjp(run_tower, kernel, up_full)
    raw_rows = text_rows[0].astype(jnp.float32)
    text_norm = jnp.sqrt(jnp.sum(raw_rows * raw_rows, axis=-1, keepdims=True) + epsilon)
    text_hat = raw_rows / text_norm
    rounded = lax.optimization_barrier(text_hat.astype(jnp.bfloat16))
    local_index = jnp.arange(img_dev, dtype=jnp.int32)

    def cycle_step(step_index, state):
        text_block, partials, image_cot = state
        source = (loop_index - step_index) % loop_size
        text_index = source * img_dev + local_index
        pair_weight = pair_grad(
            image_emb, text_block, pair_row, text_index, logit_scale, logit_bias, group_size
        )
        image_cot = image_cot + logit_scale * jnp.dot(
            pair_weight, text_block, precision=lax.Precision.HIGHEST
        )
        partials = partials + logit_scale * jnp.dot(
            pair_weight.T, image_emb, precision=lax.Precision.HIGHEST
        )
        text_block, partials = passed_along((text_block, partials), "loop", 1)
        return (text_block, partials, image_cot)

    start = (
        rounded.astype(jnp.float32),
        jnp.zeros(raw_rows.shape, jnp.float32),
        jnp.zeros(image_emb.shape, jnp.float32),
    )
    _, text_cot, image_cot = lax.fori_loop(0, loop_size, cycle_step, start)
    text_grad = (
        text_cot - text_hat * jnp.sum(text_hat * text_cot, axis=-1, keepdims=True)
    ) / text_norm
    kernel_part, up_part = pullback(image_cot)
    kernel_grad = lax.psum(kernel_part, ("loop", "dp"))
    up_rows = lax.psum_scatter(
        up_part.astype(jnp.float32).astype(jnp.bfloat16), "dp", scatter_dimension=0, tiled=True
    )
    up_grad = lax.psum(up_rows, "loop").astype(jnp.float32)
    return (kernel_grad, up_grad, text_grad[None])


def solution(mesh):
    placed = (
        P("dp", "loop", None, None, None),
        P(),
        P(),
        P("dp", None),
        P(),
        P("dp", None),
        P(),
        P("dp", None),
        P("dp", "loop", None),
        P("dp", "loop"),
        P(),
        P(),
    )
    return jax.shard_map(
        body,
        mesh=mesh,
        in_specs=placed,
        out_specs=(P(), P("dp", None), P("dp", "loop", None)),
        check_vma=False,
    )
```

profile of v0, /device:TPU:1, one launch (start us, length us, event | category | flops | bytes accessed | tf_op | source)
XLA Modules:
  0.0 996.5 jit_solution(3485320233537033907)
XLA Ops:
  15.5 30.5 %fusion.140 = (f32[2,16,16]{2,1,0:T(8,128)S(1)}, f32[2,16,16,768]{3,2,1,0:T(8,128)S(1)}) fusion(f32[768]{0:T(1024)S(1)} %get-tuple-element.377, f32[768]{0:T(1024)S(1)} %get-tuple-element.378, f32[768]{0:T(1024)S(1)} %get-tuple-element.331, f32[768]{0:T(1024)S(1)} %get-tuple-element.332, f32[768]{0:T(1024)S(1)} %get-tuple-element.333, ...), kind=kLoop, calls=%fused_computation.374 | loop fusion | flops 57802240 | bytes 2511872 | tf_op jit(solution)/shard_map/jvp()/reduce_sum | solution.py:25
  46.7 37.7 %all-gather.4.cloned.1.call-done = bf16[768,1536]{1,0:T(8,128)(2,1)} async-done(((bf16[24,1536]{1,0:T(8,128)(2,1)}), bf16[768,1536]{1,0:T(8,128)(2,1)}) %all-gather.4.cloned.1.call-update) | async-done | bytes 2359312 | tf_op jit(solution)/shard_map/all_gather | solution.py:66
  84.4 4.8 convolution_add_fusion
  89.2 65.1 %all-gather.6.cloned.1.call-done = bf16[1536,768]{1,0:T(8,128)(2,1)} async-done(((bf16[48,768]{1,0:T(8,128)(2,1)}), bf16[1536,768]{1,0:T(8,128)(2,1)}) %all-gather.6.cloned.1.call-update) | async-done | bytes 2359312 | tf_op jit(solution)/shard_map/all_gather | solution.py:67
  154.3 4.6 bitcast_reduce_fusion
  158.9 64.5 %all-gather.8.cloned.1.call-done = bf16[768,1152]{1,0:T(8,128)(2,1)} async-done(((bf16[24,1152]{1,0:T(8,128)(2,1)}), bf16[768,1152]{1,0:T(8,128)(2,1)}) %all-gather.8.cloned.1.call-update) | async-done | bytes 1769488 | tf_op jit(solution)/shard_map/all_gather | solution.py:68
  223.4 1.9 multiply_reduce_fusion.3
  225.4 184.7 %while.20 = (s32[]{:T(128)}, f32[2,1152]{1,0:T(2,128)S(1)}, f32[2,1152]{1,0:T(2,128)S(1)}, f32[2,1152]{1,0:T(2,128)S(1)}, f32[]{:T(128)}, /*index=5*/s32[1,2]{1,...) while((s32[]{:T(128)}, f32[2,1152]{1,0:T(2,128)S(1)}, ...), condition=%wide.region_6.7_spmd.clone, body=%wide.region_5.6_spmd.clone.sunk | while | flops 177470 | bytes 166336 | solution.py:110
  225.5 4.3 collective-permute-start
  230.9 3.4 collective-permute-start.1
  234.5 4.4 collective-permute-done.1
  239.0 1.9 collective-permute-start
  242.0 4.6 collective-permute-start.1
  246.8 3.2 collective-permute-done.1
  250.1 2.5 collective-permute-start
  253.7 3.4 collective-permute-start.1
  257.3 4.4 collective-permute-done.1
  261.7 1.9 collective-permute-start
  264.8 4.6 collective-permute-start.1
  269.5 3.2 collective-permute-done.1
  272.8 2.5 collective-permute-start
  276.4 3.4 collective-permute-start.1
  280.0 4.4 collective-permute-done.1
  284.4 1.9 collective-permute-start
  287.5 4.6 collective-permute-start.1
  292.3 3.2 collective-permute-done.1
  295.5 2.5 collective-permute-start
  299.1 5.2 collective-permute-start.1
  304.5 2.6 collective-permute-done.1
  307.1 3.1 collective-permute-start
  311.4 6.0 collective-permute-start.1
  319.4 3.9 collective-permute-start
  324.4 3.9 collective-permute-start.1
  328.5 4.0 collective-permute-done.1
  332.5 2.0 collective-permute-start
  335.6 3.8 collective-permute-start.1
  339.6 4.1 collective-permute-done.1
  343.7 1.9 collective-permute-start
  346.7 3.8 collective-permute-start.1
  350.7 4.1 collective-permute-done.1
  354.7 1.9 collective-permute-start
  357.8 3.8 collective-permute-start.1
  361.8 4.1 collective-permute-done.1
  365.8 1.9 collective-permute-start
  368.9 3.8 collective-permute-start.1
  372.8 4.1 collective-permute-done.1
  376.9 1.9 collective-permute-start
  380.0 3.8 collective-permute-start.1
  384.0 4.0 collective-permute-done.1
  388.0 1.9 collective-permute-start
  391.1 3.8 collective-permute-start.1
  395.0 4.1 collective-permute-done.1
  402.2 4.1 collective-permute-start.1
  406.5 3.7 collective-permute-done.1
  410.3 2.2 fusion.124
  412.6 4.6 fusion.14
  418.4 2.8 fusion.142
  421.3 3.6 fusion.143
  426.0 5.0 fusion.117
  431.1 3.7 fusion.23
  434.9 3.9 fusion.118
  440.1 119.1 %reduce-scatter.2.cloned.1.call-done = bf16[24,1536]{1,0:T(8,128)(2,1)} async-done(((bf16[768,1536]{1,0:T(8,128)(2,1)}), bf16[24,1536]{1,0:T(8,128)(2,1)}) %reduce-scatter.2.cloned.1.call-update) | async-done | bytes 73744 | tf_op jit(solution)/shard_map/reduce_scatter | solution.py:116
  560.5 148.9 %all-reduce.55.cloned.1.call-done = bf16[24,1536]{1,0:T(8,128)(2,1)} async-done(((bf16[24,1536]{1,0:T(8,128)(2,1)}), bf16[24,1536]{1,0:T(8,128)(2,1)}) %all-reduce.55.cloned.1.call-update) | async-done | bytes 73744 | tf_op jit(solution)/shard_map/psum | solution.py:119
  711.0 277.1 %all-reduce.53.cloned.1.call-done = f32[7,7,768]{2,1,0:T(8,128)} async-done(((f32[7,7,768]{2,1,0:T(8,128)}), f32[7,7,768]{2,1,0:T(8,128)}) %all-reduce.53.cloned.1.call-update) | async-done | bytes 150544 | tf_op jit(solution)/shard_map/psum | solution.py:115
  (200 shorter events, 40.7 us)
Async XLA Ops:
  7.2 77.2 %all-gather.4.cloned.1.call-start = ((), (), s32[]{:S(2)}) async-start(), calls=%async_computation.1 | async-start | bytes 2433024 | tf_op jit(solution)/shard_map/all_gather | solution.py:66
  7.9 146.4 %all-gather.6.cloned.1.call-start = ((), (), s32[]{:S(2)}) async-start(), calls=%async_computation.2 | async-start | bytes 2433024 | tf_op jit(solution)/shard_map/all_gather | solution.py:67
  8.6 214.8 %all-gather.8.cloned.1.call-start = ((), (), s32[]{:S(2)}) async-start(), calls=%async_computation.3 | async-start | bytes 1824768 | tf_op jit(solution)/shard_map/all_gather | solution.py:68
  9.4 549.9 %reduce-scatter.2.cloned.1.call-start = ((), (), s32[]{:S(2)}) async-start(), calls=%async_computation.5 | async-start | bytes 2433024 | tf_op jit(solution)/shard_map/reduce_scatter | solution.py:116
  15.5 30.9 %copy-start.1 = (f32[768]{0:T(1024)S(1)}, f32[768]{0:T(1024)}, u32[]{:S(2)}) copy-start(f32[768]{0:T(1024)} %param.16) | copy-start | bytes 9220
  46.4 38.0 %copy-start.4 = (f32[1536]{0:T(1024)S(1)}, f32[1536]{0:T(1024)}, u32[]{:S(2)}) copy-start(f32[1536]{0:T(1024)} %param.18) | copy-start | bytes 18436
  84.4 69.9 %copy-start = (bf16[1,2,16,16,768]{4,3,2,1,0:T(8,128)(2,1)S(1)}, bf16[1,2,16,16,768]{4,3,2,1,0:T(8,128)(2,1)}, u32[]{:S(2)}) copy-start(bf16[1,2,16,16,768]{4,3,2,1,0:T(8,128)(2,1)} %param.14) | copy-start | bytes 2359300
  84.4 69.9 %copy-start.2 = (f32[768]{0:T(1024)S(1)}, f32[768]{0:T(1024)}, u32[]{:S(2)}) copy-start(f32[768]{0:T(1024)} %param.20) | copy-start | bytes 9220
  158.9 66.5 %copy-start.5 = (s32[1,2]{1,0:T(1,128)S(1)}, s32[1,2]{1,0:T(1,128)}, u32[]{:S(2)}) copy-start(s32[1,2]{1,0:T(1,128)} %param.23) | copy-start | bytes 28
  225.5 13.5 %collective-permute-start = (f32[2,1152]{1,0:T(2,128)S(1)}, f32[2,1152]{1,0:T(2,128)S(1)}, u32[]{:S(2)}, u32[]{:S(2)}) collective-permute-start(f32[2,1152]{1,0:T(2,128)S(1)} %copy.20), channel_id=1, source_target_pairs={{0,32},{32,64},{64,96},{96,128},{128,160},{160,192},{192,224},{224... | collective-permute-start | bytes 27656 | tf_op jit(solution)/shard_map/while/body/eval_jaxpr/ppermute | solution.py:12
  230.9 8.0 collective-permute-start.1
  239.0 11.1 %collective-permute-start = (f32[2,1152]{1,0:T(2,128)S(1)}, f32[2,1152]{1,0:T(2,128)S(1)}, u32[]{:S(2)}, u32[]{:S(2)}) collective-permute-start(f32[2,1152]{1,0:T(2,128)S(1)} %copy.20), channel_id=1, source_target_pairs={{0,32},{32,64},{64,96},{96,128},{128,160},{160,192},{192,224},{224... | collective-permute-start | bytes 27656 | tf_op jit(solution)/shard_map/while/body/eval_jaxpr/ppermute | solution.py:12
  242.0 8.0 collective-permute-start.1
  250.1 11.6 %collective-permute-start = (f32[2,1152]{1,0:T(2,128)S(1)}, f32[2,1152]{1,0:T(2,128)S(1)}, u32[]{:S(2)}, u32[]{:S(2)}) collective-permute-start(f32[2,1152]{1,0:T(2,128)S(1)} %copy.20), channel_id=1, source_target_pairs={{0,32},{32,64},{64,96},{96,128},{128,160},{160,192},{192,224},{224... | collective-permute-start | bytes 27656 | tf_op jit(solution)/shard_map/while/body/eval_jaxpr/ppermute | solution.py:12
  253.7 8.0 collective-permute-start.1
  261.7 11.1 %collective-permute-start = (f32[2,1152]{1,0:T(2,128)S(1)}, f32[2,1152]{1,0:T(2,128)S(1)}, u32[]{:S(2)}, u32[]{:S(2)}) collective-permute-start(f32[2,1152]{1,0:T(2,128)S(1)} %copy.20), channel_id=1, source_target_pairs={{0,32},{32,64},{64,96},{96,128},{128,160},{160,192},{192,224},{224... | collective-permute-start | bytes 27656 | tf_op jit(solution)/shard_map/while/body/eval_jaxpr/ppermute | solution.py:12
  264.8 8.0 collective-permute-start.1
  272.8 11.6 %collective-permute-start = (f32[2,1152]{1,0:T(2,128)S(1)}, f32[2,1152]{1,0:T(2,128)S(1)}, u32[]{:S(2)}, u32[]{:S(2)}) collective-permute-start(f32[2,1152]{1,0:T(2,128)S(1)} %copy.20), channel_id=1, source_target_pairs={{0,32},{32,64},{64,96},{96,128},{128,160},{160,192},{192,224},{224... | collective-permute-start | bytes 27656 | tf_op jit(solution)/shard_map/while/body/eval_jaxpr/ppermute | solution.py:12
  276.4 8.0 collective-permute-start.1
  284.4 11.1 %collective-permute-start = (f32[2,1152]{1,0:T(2,128)S(1)}, f32[2,1152]{1,0:T(2,128)S(1)}, u32[]{:S(2)}, u32[]{:S(2)}) collective-permute-start(f32[2,1152]{1,0:T(2,128)S(1)} %copy.20), channel_id=1, source_target_pairs={{0,32},{32,64},{64,96},{96,128},{128,160},{160,192},{192,224},{224... | collective-permute-start | bytes 27656 | tf_op jit(solution)/shard_map/while/body/eval_jaxpr/ppermute | solution.py:12
  287.5 8.0 collective-permute-start.1
  295.5 11.6 %collective-permute-start = (f32[2,1152]{1,0:T(2,128)S(1)}, f32[2,1152]{1,0:T(2,128)S(1)}, u32[]{:S(2)}, u32[]{:S(2)}) collective-permute-start(f32[2,1152]{1,0:T(2,128)S(1)} %copy.20), channel_id=1, source_target_pairs={{0,32},{32,64},{64,96},{96,128},{128,160},{160,192},{192,224},{224... | collective-permute-start | bytes 27656 | tf_op jit(solution)/shard_map/while/body/eval_jaxpr/ppermute | solution.py:12
  299.1 8.0 collective-permute-start.1
  307.1 12.3 %collective-permute-start = (f32[2,1152]{1,0:T(2,128)S(1)}, f32[2,1152]{1,0:T(2,128)S(1)}, u32[]{:S(2)}, u32[]{:S(2)}) collective-permute-start(f32[2,1152]{1,0:T(2,128)S(1)} %copy.20), channel_id=1, source_target_pairs={{0,32},{32,64},{64,96},{96,128},{128,160},{160,192},{192,224},{224... | collective-permute-start | bytes 27656 | tf_op jit(solution)/shard_map/while/body/eval_jaxpr/ppermute | solution.py:12
  311.4 8.0 collective-permute-start.1
  319.4 13.1 %collective-permute-start = (f32[2,1152]{1,0:T(2,128)S(1)}, f32[2,1152]{1,0:T(2,128)S(1)}, u32[]{:S(2)}, u32[]{:S(2)}) collective-permute-start(f32[2,1152]{1,0:T(2,128)S(1)} %copy.20), channel_id=1, source_target_pairs={{0,32},{32,64},{64,96},{96,128},{128,160},{160,192},{192,224},{224... | collective-permute-start | bytes 27656 | tf_op jit(solution)/shard_map/while/body/eval_jaxpr/ppermute | solution.py:12
  324.4 8.0 collective-permute-start.1
  332.5 11.2 %collective-permute-start = (f32[2,1152]{1,0:T(2,128)S(1)}, f32[2,1152]{1,0:T(2,128)S(1)}, u32[]{:S(2)}, u32[]{:S(2)}) collective-permute-start(f32[2,1152]{1,0:T(2,128)S(1)} %copy.20), channel_id=1, source_target_pairs={{0,32},{32,64},{64,96},{96,128},{128,160},{160,192},{192,224},{224... | collective-permute-start | bytes 27656 | tf_op jit(solution)/shard_map/while/body/eval_jaxpr/ppermute | solution.py:12
  335.6 8.0 collective-permute-start.1
  343.7 11.1 %collective-permute-start = (f32[2,1152]{1,0:T(2,128)S(1)}, f32[2,1152]{1,0:T(2,128)S(1)}, u32[]{:S(2)}, u32[]{:S(2)}) collective-permute-start(f32[2,1152]{1,0:T(2,128)S(1)} %copy.20), channel_id=1, source_target_pairs={{0,32},{32,64},{64,96},{96,128},{128,160},{160,192},{192,224},{224... | collective-permute-start | bytes 27656 | tf_op jit(solution)/shard_map/while/body/eval_jaxpr/ppermute | solution.py:12
  346.7 8.0 collective-permute-start.1
  354.7 11.1 %collective-permute-start = (f32[2,1152]{1,0:T(2,128)S(1)}, f32[2,1152]{1,0:T(2,128)S(1)}, u32[]{:S(2)}, u32[]{:S(2)}) collective-permute-start(f32[2,1152]{1,0:T(2,128)S(1)} %copy.20), channel_id=1, source_target_pairs={{0,32},{32,64},{64,96},{96,128},{128,160},{160,192},{192,224},{224... | collective-permute-start | bytes 27656 | tf_op jit(solution)/shard_map/while/body/eval_jaxpr/ppermute | solution.py:12
  357.8 8.0 collective-permute-start.1
  365.8 11.1 %collective-permute-start = (f32[2,1152]{1,0:T(2,128)S(1)}, f32[2,1152]{1,0:T(2,128)S(1)}, u32[]{:S(2)}, u32[]{:S(2)}) collective-permute-start(f32[2,1152]{1,0:T(2,128)S(1)} %copy.20), channel_id=1, source_target_pairs={{0,32},{32,64},{64,96},{96,128},{128,160},{160,192},{192,224},{224... | collective-permute-start | bytes 27656 | tf_op jit(solution)/shard_map/while/body/eval_jaxpr/ppermute | solution.py:12
  368.9 8.0 collective-permute-start.1
  376.9 11.1 %collective-permute-start = (f32[2,1152]{1,0:T(2,128)S(1)}, f32[2,1152]{1,0:T(2,128)S(1)}, u32[]{:S(2)}, u32[]{:S(2)}) collective-permute-start(f32[2,1152]{1,0:T(2,128)S(1)} %copy.20), channel_id=1, source_target_pairs={{0,32},{32,64},{64,96},{96,128},{128,160},{160,192},{192,224},{224... | collective-permute-start | bytes 27656 | tf_op jit(solution)/shard_map/while/body/eval_jaxpr/ppermute | solution.py:12
  380.0 8.0 collective-permute-start.1
  388.0 11.1 %collective-permute-start = (f32[2,1152]{1,0:T(2,128)S(1)}, f32[2,1152]{1,0:T(2,128)S(1)}, u32[]{:S(2)}, u32[]{:S(2)}) collective-permute-start(f32[2,1152]{1,0:T(2,128)S(1)} %copy.20), channel_id=1, source_target_pairs={{0,32},{32,64},{64,96},{96,128},{128,160},{160,192},{192,224},{224... | collective-permute-start | bytes 27656 | tf_op jit(solution)/shard_map/while/body/eval_jaxpr/ppermute | solution.py:12
  391.1 8.0 collective-permute-start.1
  399.1 11.1 %collective-permute-start = (f32[2,1152]{1,0:T(2,128)S(1)}, f32[2,1152]{1,0:T(2,128)S(1)}, u32[]{:S(2)}, u32[]{:S(2)}) collective-permute-start(f32[2,1152]{1,0:T(2,128)S(1)} %copy.20), channel_id=1, source_target_pairs={{0,32},{32,64},{64,96},{96,128},{128,160},{160,192},{192,224},{224... | collective-permute-start | bytes 27656 | tf_op jit(solution)/shard_map/while/body/eval_jaxpr/ppermute | solution.py:12
  402.2 8.0 collective-permute-start.1
  410.2 2.4 copy-start.3
  417.2 1.2 copy-start.6
  421.2 288.2 %all-reduce.55.cloned.1.call-start = ((), (), s32[]{:S(2)}) async-start(), calls=%async_computation.6 | async-start | bytes 147456 | tf_op jit(solution)/shard_map/psum | solution.py:119
  559.3 428.8 %all-reduce.53.cloned.1.call-start = ((), (), s32[]{:S(2)}) async-start(), calls=%async_computation.4 | async-start | bytes 344064 | tf_op jit(solution)/shard_map/psum | solution.py:115
Sparse Core Ops, SparseCore 0:
  10.1 74.2 all-gather.3
  86.5 67.7 all-gather.5
  156.5 66.9 all-gather.7
  421.4 137.8 reduce-scatter.1
  562.0 147.3 all-reduce.54
  715.6 272.4 all-reduce.52
where the time goes:
time: 998 us; the launch traced here: 997 us
  waiting for transfers between devices  774 us (78%)
  starting transfers between devices  104 us (10%)
  other arithmetic  50 us (5%)
  matrix products  44.9 us (4%)
  between operations  15.4 us (2%)
    psum x1, waiting for transfers between devices, body(): kernel_grad = lax.psum(kernel_part, ('loop', 'dp'))  277 us
    psum x1, waiting for transfers between devices, body(): up_grad = lax.psum(up_rows, 'loop').astype(jnp.float32)  149 us
    reduce_scatter x1, waiting for transfers between devices, body(): lax.psum_scatter(up_part.astype(jnp.float32).astype(jnp.bfloat16), 'dp',...  119 us
    ppermute x32, starting transfers between devices, passed_along(): return lax.ppermute(value, axis, pairs)  104 us
    all_gather x1, waiting for transfers between devices, body(): lax.all_gather(w_down, 'dp', axis=0, tiled=True)  65.1 us
    all_gather x1, waiting for transfers between devices, body(): lax.all_gather(w_head, 'dp', axis=0, tiled=True)  64.5 us
    ppermute x32, waiting for transfers between devices, passed_along(): return lax.ppermute(value, axis, pairs)  59.5 us
    all_gather x1, waiting for transfers between devices, body(): lax.all_gather(w_up, 'dp', axis=0, tiled=True)  37.7 us
  transfers between devices with their start and end apart: 38, of which 22 were waited for; matrix products, arithmetic and copies ran while one was open for 9% of the time, Pallas kernels for 0%

commit v1 on v0

--- a/solution.py
+++ b/solution.py
@@ -116,7 +116,7 @@
     up_rows = lax.psum_scatter(
         up_part.astype(jnp.float32).astype(jnp.bfloat16), "dp", scatter_dimension=0, tiled=True
     )
-    up_grad = lax.psum(up_rows, "loop").astype(jnp.float32)
+    up_grad = jnp.sum(lax.all_gather(up_rows, "loop"), axis=0).astype(jnp.float32)
     return (kernel_grad, up_grad, text_grad[None])
 
 

time: 998 us -> 925 us (0.927)
  waiting for transfers between devices: 774 us -> 700 us
    psum x1 -> x0, waiting for transfers between devices: 149 us -> none  [body(): up_grad = lax.psum(up_rows, 'loop').astype(jnp.float32)]
    all_gather x0 -> x1, waiting for transfers between devices: none -> 70.3 us  [body(): lax.all_gather(up_rows, 'loop')]
    reduce_scatter x1, waiting for transfers between devices: 119 us -> 133 us  [body(): lax.psum_scatter(up_part.astype(jnp.float32).astype(jnp.bfloat16), 'dp',...]
where the time goes in v1:
time: 925 us; the launch traced here: 923 us
  waiting for transfers between devices  700 us (76%)
  starting transfers between devices  104 us (11%)
  other arithmetic  50.6 us (5%)
  matrix products  44.9 us (5%)
  between operations  15.4 us (2%)
    psum x1, waiting for transfers between devices, body(): kernel_grad = lax.psum(kernel_part, ('loop', 'dp'))  268 us
    reduce_scatter x1, waiting for transfers between devices, body(): lax.psum_scatter(up_part.astype(jnp.float32).astype(jnp.bfloat16), 'dp',...  133 us
    ppermute x32, starting transfers between devices, passed_along(): return lax.ppermute(value, axis, pairs)  104 us
    all_gather x1, waiting for transfers between devices, body(): lax.all_gather(up_rows, 'loop')  70.3 us
    all_gather x1, waiting for transfers between devices, body(): lax.all_gather(w_down, 'dp', axis=0, tiled=True)  65.1 us
    all_gather x1, waiting for transfers between devices, body(): lax.all_gather(w_head, 'dp', axis=0, tiled=True)  64.5 us
    ppermute x32, waiting for transfers between devices, passed_along(): return lax.ppermute(value, axis, pairs)  59.4 us
    all_gather x1, waiting for transfers between devices, body(): lax.all_gather(w_up, 'dp', axis=0, tiled=True)  37.7 us
  transfers between devices with their start and end apart: 38, of which 22 were waited for; matrix products, arithmetic and copies ran while one was open for 9% of the time, Pallas kernels for 0%

profile of v1, /device:TPU:1, one launch (start us, length us, event | category | flops | bytes accessed | tf_op | source)
XLA Modules:
  0.0 923.1 jit_solution(6364706673033407913)
XLA Ops:
  15.5 30.5 %fusion.140 = (f32[2,16,16]{2,1,0:T(8,128)S(1)}, f32[2,16,16,768]{3,2,1,0:T(8,128)S(1)}) fusion(f32[768]{0:T(1024)S(1)} %get-tuple-element.377, f32[768]{0:T(1024)S(1)} %get-tuple-element.378, f32[768]{0:T(1024)S(1)} %get-tuple-element.331, f32[768]{0:T(1024)S(1)} %get-tuple-element.332, f32[768]{0:T(1024)S(1)} %get-tuple-element.333, ...), kind=kLoop, calls=%fused_computation.374 | loop fusion | flops 57802240 | bytes 2511872 | tf_op jit(solution)/shard_map/jvp()/reduce_sum | solution.py:25
  46.7 37.7 %all-gather.6.cloned.1.call-done = bf16[768,1536]{1,0:T(8,128)(2,1)} async-done(((bf16[24,1536]{1,0:T(8,128)(2,1)}), bf16[768,1536]{1,0:T(8,128)(2,1)}) %all-gather.6.cloned.1.call-update) | async-done | bytes 2359312 | tf_op jit(solution)/shard_map/all_gather | solution.py:66
  84.4 4.8 convolution_add_fusion
  89.2 65.1 %all-gather.8.cloned.1.call-done = bf16[1536,768]{1,0:T(8,128)(2,1)} async-done(((bf16[48,768]{1,0:T(8,128)(2,1)}), bf16[1536,768]{1,0:T(8,128)(2,1)}) %all-gather.8.cloned.1.call-update) | async-done | bytes 2359312 | tf_op jit(solution)/shard_map/all_gather | solution.py:67
  154.3 4.6 bitcast_reduce_fusion
  158.9 64.5 %all-gather.10.cloned.1.call-done = bf16[768,1152]{1,0:T(8,128)(2,1)} async-done(((bf16[24,1152]{1,0:T(8,128)(2,1)}), bf16[768,1152]{1,0:T(8,128)(2,1)}) %all-gather.10.cloned.1.call-update) | async-done | bytes 1769488 | tf_op jit(solution)/shard_map/all_gather | solution.py:68
  223.4 1.9 multiply_reduce_fusion.3
  225.4 184.7 %while.20 = (s32[]{:T(128)}, f32[2,1152]{1,0:T(2,128)S(1)}, f32[2,1152]{1,0:T(2,128)S(1)}, f32[2,1152]{1,0:T(2,128)S(1)}, f32[]{:T(128)}, /*index=5*/s32[1,2]{1,...) while((s32[]{:T(128)}, f32[2,1152]{1,0:T(2,128)S(1)}, ...), condition=%wide.region_6.7_spmd.clone, body=%wide.region_5.6_spmd.clone.sunk | while | flops 177470 | bytes 166336 | solution.py:110
  225.5 4.3 collective-permute-start
  230.9 3.4 collective-permute-start.1
  234.5 4.4 collective-permute-done.1
  239.0 1.9 collective-permute-start
  242.0 4.6 collective-permute-start.1
  246.8 3.2 collective-permute-done.1
  250.1 2.5 collective-permute-start
  253.7 3.4 collective-permute-start.1
  257.3 4.4 collective-permute-done.1
  261.7 1.9 collective-permute-start
  264.8 4.6 collective-permute-start.1
  269.5 3.2 collective-permute-done.1
  272.8 2.5 collective-permute-start
  276.4 3.4 collective-permute-start.1
  280.0 4.4 collective-permute-done.1
  284.4 1.9 collective-permute-start
  287.5 4.6 collective-permute-start.1
  292.3 3.2 collective-permute-done.1
  295.5 2.5 collective-permute-start
  299.1 5.2 collective-permute-start.1
  304.5 2.6 collective-permute-done.1
  307.1 3.1 collective-permute-start
  311.4 6.0 collective-permute-start.1
  319.4 3.9 collective-permute-start
  324.4 3.9 collective-permute-start.1
  328.5 4.0 collective-permute-done.1
  332.5 2.0 collective-permute-start
  335.6 3.8 collective-permute-start.1
  339.6 4.0 collective-permute-done.1
  343.6 1.9 collective-permute-start
  346.7 3.8 collective-permute-start.1
  350.7 4.1 collective-permute-done.1
  354.7 1.9 collective-permute-start
  357.8 3.8 collective-permute-start.1
  361.8 4.1 collective-permute-done.1
  365.8 1.9 collective-permute-start
  368.9 3.8 collective-permute-start.1
  372.8 4.0 collective-permute-done.1
  376.9 1.9 collective-permute-start
  380.0 3.8 collective-permute-start.1
  384.0 4.0 collective-permute-done.1
  388.0 1.9 collective-permute-start
  391.1 3.8 collective-permute-start.1
  395.0 4.0 collective-permute-done.1
  402.1 4.1 collective-permute-start.1
  406.5 3.7 collective-permute-done.1
  410.3 2.2 fusion.124
  412.6 4.6 fusion.14
  418.4 2.8 fusion.142
  421.3 3.6 fusion.143
  425.9 133.3 %reduce-scatter.2.cloned.1.call-done = bf16[24,1536]{1,0:T(8,128)(2,1)} async-done(((bf16[768,1536]{1,0:T(8,128)(2,1)}), bf16[24,1536]{1,0:T(8,128)(2,1)}) %reduce-scatter.2.cloned.1.call-update) | async-done | bytes 73744 | tf_op jit(solution)/shard_map/reduce_scatter | solution.py:116
  559.4 5.0 fusion.117
  564.5 3.7 fusion.23
  568.3 3.9 fusion.118
  574.4 70.3 %all-gather.12.cloned.1.call-done = bf16[384,1536]{1,0:T(8,128)(2,1)} async-done(((bf16[24,1536]{1,0:T(8,128)(2,1)}), bf16[384,1536]{1,0:T(8,128)(2,1)}) %all-gather.12.cloned.1.call-update) | async-done | bytes 1179664 | tf_op jit(solution)/shard_map/all_gather | solution.py:119
  646.8 267.8 %all-reduce.52.cloned.1.call-done = f32[7,7,768]{2,1,0:T(8,128)} async-done(((f32[7,7,768]{2,1,0:T(8,128)}), f32[7,7,768]{2,1,0:T(8,128)}) %all-reduce.52.cloned.1.call-update) | async-done | bytes 150544 | tf_op jit(solution)/shard_map/psum | solution.py:115
  (201 shorter events, 40.8 us)
Async XLA Ops:
  7.2 77.2 %all-gather.6.cloned.1.call-start = ((), (), s32[]{:S(2)}) async-start(), calls=%async_computation.1 | async-start | bytes 2433024 | tf_op jit(solution)/shard_map/all_gather | solution.py:66
  7.9 146.4 %all-gather.8.cloned.1.call-start = ((), (), s32[]{:S(2)}) async-start(), calls=%async_computation.2 | async-start | bytes 2433024 | tf_op jit(solution)/shard_map/all_gather | solution.py:67
  8.6 214.8 %all-gather.10.cloned.1.call-start = ((), (), s32[]{:S(2)}) async-start(), calls=%async_computation.3 | async-start | bytes 1824768 | tf_op jit(solution)/shard_map/all_gather | solution.py:68
  9.4 549.9 %reduce-scatter.2.cloned.1.call-start = ((), (), s32[]{:S(2)}) async-start(), calls=%async_computation.5 | async-start | bytes 2433024 | tf_op jit(solution)/shard_map/reduce_scatter | solution.py:116
  15.5 30.8 %copy-start.1 = (f32[768]{0:T(1024)S(1)}, f32[768]{0:T(1024)}, u32[]{:S(2)}) copy-start(f32[768]{0:T(1024)} %param.16) | copy-start | bytes 9220
  46.3 38.1 %copy-start.4 = (f32[1536]{0:T(1024)S(1)}, f32[1536]{0:T(1024)}, u32[]{:S(2)}) copy-start(f32[1536]{0:T(1024)} %param.18) | copy-start | bytes 18436
  84.4 69.9 %copy-start = (bf16[1,2,16,16,768]{4,3,2,1,0:T(8,128)(2,1)S(1)}, bf16[1,2,16,16,768]{4,3,2,1,0:T(8,128)(2,1)}, u32[]{:S(2)}) copy-start(bf16[1,2,16,16,768]{4,3,2,1,0:T(8,128)(2,1)} %param.14) | copy-start | bytes 2359300
  84.4 69.9 %copy-start.2 = (f32[768]{0:T(1024)S(1)}, f32[768]{0:T(1024)}, u32[]{:S(2)}) copy-start(f32[768]{0:T(1024)} %param.20) | copy-start | bytes 9220
  158.9 66.5 %copy-start.5 = (s32[1,2]{1,0:T(1,128)S(1)}, s32[1,2]{1,0:T(1,128)}, u32[]{:S(2)}) copy-start(s32[1,2]{1,0:T(1,128)} %param.23) | copy-start | bytes 28
  225.5 13.5 %collective-permute-start = (f32[2,1152]{1,0:T(2,128)S(1)}, f32[2,1152]{1,0:T(2,128)S(1)}, u32[]{:S(2)}, u32[]{:S(2)}) collective-permute-start(f32[2,1152]{1,0:T(2,128)S(1)} %copy.20), channel_id=1, source_target_pairs={{0,32},{32,64},{64,96},{96,128},{128,160},{160,192},{192,224},{224... | collective-permute-start | bytes 27656 | tf_op jit(solution)/shard_map/while/body/eval_jaxpr/ppermute | solution.py:12
  230.9 8.0 collective-permute-start.1
  239.0 11.1 %collective-permute-start = (f32[2,1152]{1,0:T(2,128)S(1)}, f32[2,1152]{1,0:T(2,128)S(1)}, u32[]{:S(2)}, u32[]{:S(2)}) collective-permute-start(f32[2,1152]{1,0:T(2,128)S(1)} %copy.20), channel_id=1, source_target_pairs={{0,32},{32,64},{64,96},{96,128},{128,160},{160,192},{192,224},{224... | collective-permute-start | bytes 27656 | tf_op jit(solution)/shard_map/while/body/eval_jaxpr/ppermute | solution.py:12
  242.0 8.0 collective-permute-start.1
  250.1 11.6 %collective-permute-start = (f32[2,1152]{1,0:T(2,128)S(1)}, f32[2,1152]{1,0:T(2,128)S(1)}, u32[]{:S(2)}, u32[]{:S(2)}) collective-permute-start(f32[2,1152]{1,0:T(2,128)S(1)} %copy.20), channel_id=1, source_target_pairs={{0,32},{32,64},{64,96},{96,128},{128,160},{160,192},{192,224},{224... | collective-permute-start | bytes 27656 | tf_op jit(solution)/shard_map/while/body/eval_jaxpr/ppermute | solution.py:12
  253.7 8.0 collective-permute-start.1
  261.7 11.1 %collective-permute-start = (f32[2,1152]{1,0:T(2,128)S(1)}, f32[2,1152]{1,0:T(2,128)S(1)}, u32[]{:S(2)}, u32[]{:S(2)}) collective-permute-start(f32[2,1152]{1,0:T(2,128)S(1)} %copy.20), channel_id=1, source_target_pairs={{0,32},{32,64},{64,96},{96,128},{128,160},{160,192},{192,224},{224... | collective-permute-start | bytes 27656 | tf_op jit(solution)/shard_map/while/body/eval_jaxpr/ppermute | solution.py:12
  264.8 8.0 collective-permute-start.1
  272.8 11.6 %collective-permute-start = (f32[2,1152]{1,0:T(2,128)S(1)}, f32[2,1152]{1,0:T(2,128)S(1)}, u32[]{:S(2)}, u32[]{:S(2)}) collective-permute-start(f32[2,1152]{1,0:T(2,128)S(1)} %copy.20), channel_id=1, source_target_pairs={{0,32},{32,64},{64,96},{96,128},{128,160},{160,192},{192,224},{224... | collective-permute-start | bytes 27656 | tf_op jit(solution)/shard_map/while/body/eval_jaxpr/ppermute | solution.py:12
  276.4 8.0 collective-permute-start.1
  284.4 11.1 %collective-permute-start = (f32[2,1152]{1,0:T(2,128)S(1)}, f32[2,1152]{1,0:T(2,128)S(1)}, u32[]{:S(2)}, u32[]{:S(2)}) collective-permute-start(f32[2,1152]{1,0:T(2,128)S(1)} %copy.20), channel_id=1, source_target_pairs={{0,32},{32,64},{64,96},{96,128},{128,160},{160,192},{192,224},{224... | collective-permute-start | bytes 27656 | tf_op jit(solution)/shard_map/while/body/eval_jaxpr/ppermute | solution.py:12
  287.5 8.0 collective-permute-start.1
  295.5 11.6 %collective-permute-start = (f32[2,1152]{1,0:T(2,128)S(1)}, f32[2,1152]{1,0:T(2,128)S(1)}, u32[]{:S(2)}, u32[]{:S(2)}) collective-permute-start(f32[2,1152]{1,0:T(2,128)S(1)} %copy.20), channel_id=1, source_target_pairs={{0,32},{32,64},{64,96},{96,128},{128,160},{160,192},{192,224},{224... | collective-permute-start | bytes 27656 | tf_op jit(solution)/shard_map/while/body/eval_jaxpr/ppermute | solution.py:12
  299.1 8.0 collective-permute-start.1
  307.1 12.2 %collective-permute-start = (f32[2,1152]{1,0:T(2,128)S(1)}, f32[2,1152]{1,0:T(2,128)S(1)}, u32[]{:S(2)}, u32[]{:S(2)}) collective-permute-start(f32[2,1152]{1,0:T(2,128)S(1)} %copy.20), channel_id=1, source_target_pairs={{0,32},{32,64},{64,96},{96,128},{128,160},{160,192},{192,224},{224... | collective-permute-start | bytes 27656 | tf_op jit(solution)/shard_map/while/body/eval_jaxpr/ppermute | solution.py:12
  311.4 8.0 collective-permute-start.1
  319.4 13.1 %collective-permute-start = (f32[2,1152]{1,0:T(2,128)S(1)}, f32[2,1152]{1,0:T(2,128)S(1)}, u32[]{:S(2)}, u32[]{:S(2)}) collective-permute-start(f32[2,1152]{1,0:T(2,128)S(1)} %copy.20), channel_id=1, source_target_pairs={{0,32},{32,64},{64,96},{96,128},{128,160},{160,192},{192,224},{224... | collective-permute-start | bytes 27656 | tf_op jit(solution)/shard_map/while/body/eval_jaxpr/ppermute | solution.py:12
  324.4 8.0 collective-permute-start.1
  332.5 11.2 %collective-permute-start = (f32[2,1152]{1,0:T(2,128)S(1)}, f32[2,1152]{1,0:T(2,128)S(1)}, u32[]{:S(2)}, u32[]{:S(2)}) collective-permute-start(f32[2,1152]{1,0:T(2,128)S(1)} %copy.20), channel_id=1, source_target_pairs={{0,32},{32,64},{64,96},{96,128},{128,160},{160,192},{192,224},{224... | collective-permute-start | bytes 27656 | tf_op jit(solution)/shard_map/while/body/eval_jaxpr/ppermute | solution.py:12
  335.6 8.0 collective-permute-start.1
  343.6 11.1 %collective-permute-start = (f32[2,1152]{1,0:T(2,128)S(1)}, f32[2,1152]{1,0:T(2,128)S(1)}, u32[]{:S(2)}, u32[]{:S(2)}) collective-permute-start(f32[2,1152]{1,0:T(2,128)S(1)} %copy.20), channel_id=1, source_target_pairs={{0,32},{32,64},{64,96},{96,128},{128,160},{160,192},{192,224},{224... | collective-permute-start | bytes 27656 | tf_op jit(solution)/shard_map/while/body/eval_jaxpr/ppermute | solution.py:12
  346.7 8.0 collective-permute-start.1
  354.7 11.1 %collective-permute-start = (f32[2,1152]{1,0:T(2,128)S(1)}, f32[2,1152]{1,0:T(2,128)S(1)}, u32[]{:S(2)}, u32[]{:S(2)}) collective-permute-start(f32[2,1152]{1,0:T(2,128)S(1)} %copy.20), channel_id=1, source_target_pairs={{0,32},{32,64},{64,96},{96,128},{128,160},{160,192},{192,224},{224... | collective-permute-start | bytes 27656 | tf_op jit(solution)/shard_map/while/body/eval_jaxpr/ppermute | solution.py:12
  357.8 8.0 collective-permute-start.1
  365.8 11.1 %collective-permute-start = (f32[2,1152]{1,0:T(2,128)S(1)}, f32[2,1152]{1,0:T(2,128)S(1)}, u32[]{:S(2)}, u32[]{:S(2)}) collective-permute-start(f32[2,1152]{1,0:T(2,128)S(1)} %copy.20), channel_id=1, source_target_pairs={{0,32},{32,64},{64,96},{96,128},{128,160},{160,192},{192,224},{224... | collective-permute-start | bytes 27656 | tf_op jit(solution)/shard_map/while/body/eval_jaxpr/ppermute | solution.py:12
  368.9 8.0 collective-permute-start.1
  376.9 11.1 %collective-permute-start = (f32[2,1152]{1,0:T(2,128)S(1)}, f32[2,1152]{1,0:T(2,128)S(1)}, u32[]{:S(2)}, u32[]{:S(2)}) collective-permute-start(f32[2,1152]{1,0:T(2,128)S(1)} %copy.20), channel_id=1, source_target_pairs={{0,32},{32,64},{64,96},{96,128},{128,160},{160,192},{192,224},{224... | collective-permute-start | bytes 27656 | tf_op jit(solution)/shard_map/while/body/eval_jaxpr/ppermute | solution.py:12
  380.0 8.0 collective-permute-start.1
  388.0 11.1 %collective-permute-start = (f32[2,1152]{1,0:T(2,128)S(1)}, f32[2,1152]{1,0:T(2,128)S(1)}, u32[]{:S(2)}, u32[]{:S(2)}) collective-permute-start(f32[2,1152]{1,0:T(2,128)S(1)} %copy.20), channel_id=1, source_target_pairs={{0,32},{32,64},{64,96},{96,128},{128,160},{160,192},{192,224},{224... | collective-permute-start | bytes 27656 | tf_op jit(solution)/shard_map/while/body/eval_jaxpr/ppermute | solution.py:12
  391.1 8.0 collective-permute-start.1
  399.1 11.1 %collective-permute-start = (f32[2,1152]{1,0:T(2,128)S(1)}, f32[2,1152]{1,0:T(2,128)S(1)}, u32[]{:S(2)}, u32[]{:S(2)}) collective-permute-start(f32[2,1152]{1,0:T(2,128)S(1)} %copy.20), channel_id=1, source_target_pairs={{0,32},{32,64},{64,96},{96,128},{128,160},{160,192},{192,224},{224... | collective-permute-start | bytes 27656 | tf_op jit(solution)/shard_map/while/body/eval_jaxpr/ppermute | solution.py:12
  402.1 8.0 collective-permute-start.1
  410.2 2.4 copy-start.3
  417.2 1.2 copy-start.6
  421.2 223.5 %all-gather.12.cloned.1.call-start = ((), (), s32[]{:S(2)}) async-start(), calls=%async_computation.6 | async-start | bytes 1253376 | tf_op jit(solution)/shard_map/all_gather | solution.py:119
  559.3 355.3 %all-reduce.52.cloned.1.call-start = ((), (), s32[]{:S(2)}) async-start(), calls=%async_computation.4 | async-start | bytes 344064 | tf_op jit(solution)/shard_map/psum | solution.py:115
Sparse Core Ops, SparseCore 0:
  10.1 74.2 all-gather.5
  86.5 67.7 all-gather.7
  156.5 66.9 all-gather.9
  421.3 137.8 reduce-scatter.1
  562.3 82.3 all-gather.11
  650.1 264.4 all-reduce.51
